TPU v7x, 512 devices: a whole 4x4x16 slice. The times are simulated.
512 devices in a mesh: vocab: 128 (over x, z, core), batch: 4 (over y).
Axes of the slice: x: 4, y: 4, z: 16, core: 2. Of those that a mesh axis runs over, the one named last changes fastest.
Arguments:
- hidden: bfloat16 [4096, 1024], P(('vocab', 'batch'))
- embedding: bfloat16 [131072, 1024], P('vocab')
- block_counts: int32 [1024], P('vocab'), may hold values from 1 to 4095
- lang_blocks: int32 [200, 64], replicated, may hold values from -1 to 1023, as said below
- sent_lang: int32 [64], replicated, may hold values from 0 to 199
- targets: int32 [4096], replicated, may hold values from 0 to 131071, as said below
Outputs:
- token_loss: float32 [4096], P(('vocab', 'batch'))
- grad_embed: bfloat16 [131072, 1024], P(('vocab', 'batch'))
Inputs may be any that keep to these rules, and one draw needn't show every extreme that they name: `lang_blocks`: each list holds distinct block numbers and then -1 padding; the first entry of every list is block 0; at least 16 entries are blocks, and some language fills all 64 entries. `targets`: the target of token t lies in a block listed for the language of sentence t // 64.
All inputs are finite; a program needn't handle non-finite values.
Results may differ from a plain program's by a relative error of at most 0.0075.
Values may be sent and summed in bfloat16 or wider, within the bound.
A program may use at most 64 MiB of HBM per device.

v0:
```python
import jax
import jax.numpy as jnp
from jax import lax
from jax.sharding import PartitionSpec as P

SEQ = 64


masked_fill = -1e30


def body(hidden, embedding, block_counts, lang_blocks, sent_lang, targets):
    tok_dev = hidden.shape[0]
    vocab_count = lax.axis_size("vocab")
    batch_count = lax.axis_size("batch")
    vocab_index = lax.axis_index("vocab")
    batch_index = lax.axis_index("batch")
    local_rows = embedding.shape[0]
    local_blocks = block_counts.shape[0]
    block_width = local_rows // local_blocks
    gathered = lax.all_gather(hidden, "vocab", axis=0, tiled=True)
    token_count = gathered.shape[0]
    token_ids = (
        (jnp.arange(vocab_count, dtype=jnp.int32)[:, None] * batch_count + batch_index) * tok_dev
        + jnp.arange(tok_dev, dtype=jnp.int32)[None, :]
    ).reshape(-1)
    target_ids = lax.dynamic_index_in_dim(
        targets.reshape(vocab_count, batch_count, tok_dev), batch_index, 1, keepdims=False
    ).reshape(-1)
    sentence = token_ids // SEQ
    sentence_hit = sentence[:, None] == jnp.arange(sent_lang.shape[0], dtype=jnp.int32)[None, :]
    token_language = jnp.sum(jnp.where(sentence_hit, sent_lang[None, :], 0), axis=1)
    block_ids = vocab_index * local_blocks + jnp.arange(local_blocks, dtype=jnp.int32)
    member = jnp.any(lang_blocks[:, :, None] == block_ids[None, None, :], axis=1).astype(
        jnp.float32
    )
    language_hit = (
        token_language[:, None] == jnp.arange(lang_blocks.shape[0], dtype=jnp.int32)[None, :]
    ).astype(jnp.float32)
    allowed = jnp.dot(language_hit, member, precision=lax.Precision.HIGHEST) > 0.5
    allowed_cells = allowed[:, :, None]
    raw_scores = lax.dot_general(
        gathered, embedding, (((1,), (1,)), ((), ())), preferred_element_type=jnp.float32
    )
    log_sampling = jnp.log(block_counts.astype(jnp.float32))
    logits = (
        raw_scores.reshape(token_count, local_blocks, block_width) - log_sampling[None, :, None]
    )
    masked = jnp.where(allowed_cells, logits, masked_fill)
    word_ids = (vocab_index * local_rows + jnp.arange(local_rows, dtype=jnp.int32)).reshape(
        local_blocks, block_width
    )
    is_target = word_ids[None, :, :] == target_ids[:, None, None]
    local_peak = jnp.max(masked, axis=(1, 2))
    local_target = jnp.sum(jnp.where(is_target, logits, 0.0), axis=(1, 2))
    peak_value = lax.pmax(local_peak, "vocab")
    local_total = jnp.sum(
        jnp.where(allowed_cells, jnp.exp(masked - peak_value[:, None, None]), 0.0), axis=(1, 2)
    )
    denominator, target_logit = lax.psum((local_total, local_target), "vocab")
    log_total = peak_value + jnp.log(denominator)
    every_loss = log_total - target_logit
    token_loss = lax.dynamic_slice_in_dim(every_loss, vocab_index * tok_dev, tok_dev, 0)
    softmax_weights = jnp.where(allowed_cells, jnp.exp(logits - log_total[:, None, None]), 0.0)
    grad_logits = (
        (softmax_weights - is_target.astype(jnp.float32))
        .astype(jnp.bfloat16)
        .reshape(token_count, local_rows)
    )
    partial_value = lax.dot_general(
        grad_logits, gathered, (((0,), (0,)), ((), ())), preferred_element_type=jnp.float32
    )
    rounded_terms = partial_value.astype(jnp.bfloat16)
    grad_embed = (
        lax.psum_scatter(rounded_terms, "batch", scatter_dimension=0, tiled=True)
        .astype(jnp.float32)
        .astype(jnp.bfloat16)
    )
    return (token_loss, grad_embed)


def solution(mesh):
    in_specs = (P(("vocab", "batch"), None), P("vocab", None), P("vocab"), P(), P(), P())
    out_specs = (P(("vocab", "batch")), P(("vocab", "batch"), None))
    return jax.shard_map(body, mesh=mesh, in_specs=in_specs, out_specs=out_specs, check_vma=False)
```

profile of v0, /device:TPU:1, one launch (start us, length us, event | category | flops | bytes accessed | tf_op | source)
XLA Modules:
  0.0 706.7 jit_solution(17756853080807426681)
XLA Ops:
  7.2 0.0 copy-start
  7.2 0.0 all-gather.2.cloned.1.call-start
  7.2 0.7 all-gather.2.cloned.1.call-update
  7.9 0.0 reduce-scatter.2.cloned.1.call-start
  8.0 0.1 iota_add_fusion
  8.1 0.1 add.86
  8.2 1.1 reshape.84
  9.2 0.2 dynamic-slice_reduce_fusion
  9.4 0.1 eq.66
  9.6 0.8 select_reduce_fusion
  10.3 1.0 compare_reduce_fusion
  11.3 0.7 convert_log_fusion
  12.0 0.1 broadcast_bitcast_fusion
  12.1 0.4 convolution_compare_fusion
  12.4 144.3 %all-gather.2.cloned.1.call-done = bf16[1024,1024]{1,0:T(8,128)(2,1)} async-done(((bf16[8,1024]{1,0:T(8,128)(2,1)}), bf16[1024,1024]{1,0:T(8,128)(2,1)}) %all-gather.2.cloned.1.call-update) | async-done | bytes 2097168 | tf_op jit(solution)/shard_map/all_gather | solution.py:21
  156.7 0.0 copy-done
  156.7 5.9 fusion.4
  162.6 246.4 %pmax.7 = f32[1024]{0:T(1024)S(1)} all-reduce(f32[1024]{0:T(1024)S(1)} %get-tuple-element.8), channel_id=1, replica_groups=mesh['vocab'=128,'batch'=4] {'vocab'}, use_global_device_ids=true, to_apply=%region_3.4 | all-reduce | flops 1024 | bytes 8192 | tf_op jit(solution)/shard_map/pmax | solution.py:56
  409.0 3.3 fusion
  412.3 254.4 %all-reduce = (f32[1024]{0:T(1024)S(1)}, f32[1024]{0:T(1024)S(1)}) all-reduce(f32[1024]{0:T(1024)S(1)} %get-tuple-element.3, f32[1024]{0:T(1024)S(1)} %get-tuple-element.2), channel_id=1, replica_groups=mesh['vocab'=128,'batch'=4] {'vocab'}, use_global_device_ids=true, to_apply=%region_5.6 | all-reduce | flops 2048 | bytes 16384 | tf_op jit(solution)/shard_map/psum | solution.py:60
  666.7 0.0 copy-start.1
  666.7 3.2 fusion.2
  669.9 0.0 copy-done.1
  669.9 3.7 convolution_convert_fusion
  673.6 0.0 reduce-scatter.2.cloned.1.call-update
  673.7 0.6 dynamic_slice.8
  674.3 25.6 %reduce-scatter.2.cloned.1.call-done = bf16[256,1024]{1,0:T(8,128)(2,1)} async-done(((bf16[1024,1024]{1,0:T(8,128)(2,1)}), bf16[256,1024]{1,0:T(8,128)(2,1)}) %reduce-scatter.2.cloned.1.call-update) | async-done | bytes 524304 | tf_op jit(solution)/shard_map/reduce_scatter | solution.py:75
  (5 shorter events, 0.0 us)
Async XLA Ops:
  7.2 149.5 %copy-start = (bf16[1024,1024]{1,0:T(8,128)(2,1)S(1)}, bf16[1024,1024]{1,0:T(8,128)(2,1)}, u32[]{:S(2)}) copy-start(bf16[1024,1024]{1,0:T(8,128)(2,1)} %param.7) | copy-start | bytes 6291460
  7.2 149.5 %all-gather.2.cloned.1.call-start = ((), (), s32[]{:S(2)}) async-start(), calls=%async_computation.1 | async-start | bytes 2113536 | tf_op jit(solution)/shard_map/all_gather | solution.py:21
  7.9 691.9 %reduce-scatter.2.cloned.1.call-start = ((), (), s32[]{:S(2)}) async-start(), calls=%async_computation.2 | async-start | bytes 2621440 | tf_op jit(solution)/shard_map/reduce_scatter | solution.py:75
  666.7 3.2 copy-start.1
Sparse Core Ops, SparseCore 0:
  11.1 145.4 all-gather.1
  673.8 26.0 reduce-scatter.1
where the time goes:
time: 707 us
  blocking collectives  501 us (71%)
  waiting for transfers between devices  171 us (24%)
  between operations  14.2 us (2%)
  matrix products  9.95 us (1%)
  other arithmetic  9.04 us (1%)
    psum x1, blocking collectives, body(): denominator, target_logit = lax.psum((local_total, local_target), 'vocab')  254 us
    pmax x1, blocking collectives, body(): peak_value = lax.pmax(local_peak, 'vocab')  246 us
    all_gather x1, waiting for transfers between devices, body(): gathered = lax.all_gather(hidden, 'vocab', axis=0, tiled=True)  144 us
    reduce_scatter x1, waiting for transfers between devices, body(): lax.psum_scatter(rounded_terms, 'batch', scatter_dimension=0, tiled=True)  25.6 us
  transfers between devices with their start and end apart: 2, of which 2 were waited for; matrix products, arithmetic and copies ran while one was open for 1% of the time, Pallas kernels for 0%

commit v1 on v0

v1 whole, which is shorter than its diff:
```python
import functools

import jax
import jax.numpy as jnp
from jax import lax
from jax.experimental import pallas as pl
from jax.experimental.pallas import tpu as pltpu
from jax.sharding import PartitionSpec as P

MESH = pl.DeviceIdType.MESH
F32, BF16 = jnp.float32, jnp.bfloat16
NX, NZ, NY = 4, 16, 4
D = 1024
HALF = 512
ROWS = 1024
TOK = 1024
NB = 8
BLK = 128
QROWS = 256
CHUNK = 256
FILL = -3e38
REACH = 4
ZORDER = [0] + [s * k for k in range(1, 8) for s in (1, -1)] + [-8]
XPEERS = (1, 3, 2)


def remote(src, dst, send, recv, device):
    return pltpu.make_async_remote_copy(
        src_ref=src, dst_ref=dst, send_sem=send, recv_sem=recv,
        device_id=device, device_id_type=MESH,
    )


def merge(parts):
    top = functools.reduce(jnp.maximum, parts)
    total = functools.reduce(jnp.add, [jnp.exp(p - top) for p in parts])
    return top + jnp.log(total)


def kernel(
    hid_ref, emb_ref, counts_ref, lists_ref, lane_ref,
    loss_ref, grad_ref,
    table, tokens, logits, probs, swap, allowed, peak_row, total_row,
    s1, s2, t1, t2, lse_out, l1_out, tgt_out, tsum_out, send_buf, recv_buf, out_buf,
    sem_table, sem_swap, sem_z_send, sem_z, sem_x_send, sem_x, sem_c_send, sem_c,
    sem_s1s, sem_s1, sem_s2s, sem_s2, sem_t1s, sem_t1, sem_t2s, sem_t2, sem_rs, sem_rr,
    sem_out,
):
    v, y = lax.axis_index("vocab"), lax.axis_index("batch")
    c = lax.rem(v, 2)
    z = lax.rem(lax.div(v, 2), NZ)
    x = lax.div(v, 2 * NZ)

    def dev(px, pz, pc, py):
        return {"vocab": (px * NZ + pz) * 2 + pc, "batch": py}

    def at_z(k):
        return dev(x, lax.rem(z + k + 2 * NZ, NZ), c, y)

    def at_x(k, flip=0):
        return dev(lax.rem(x + k, NX), z, (1 - c) if flip else c, y)

    partner = dev(x, z, 1 - c, y)
    xc_peers = [(k, f) for f in (0, 1) for k in range(NX) if (k, f) != (0, 0)]

    load = pltpu.make_async_copy(emb_ref, table, sem_table)
    load.start()

    barrier = pltpu.get_barrier_semaphore()
    near = [at_x(k, f) for k, f in xc_peers]
    near += [at_z(s * k) for k in range(1, REACH + 1) for s in (1, -1)]
    near += [dev(x, z, c, lax.rem(y + k, NY)) for k in range(1, NY)]
    for peer in near:
        pl.semaphore_signal(barrier, inc=1, device_id=peer, device_id_type=MESH)
    pl.semaphore_wait(barrier, len(near))

    mine = hid_ref[...].astype(F32)
    low, high = mine[:, :HALF], mine[:, HALF:]
    swap[0] = jnp.where(c == 0, high, low)
    trade = remote(swap.at[0], swap.at[1], sem_swap.at[0], sem_swap.at[1], partner)
    trade.start()

    lists = lists_ref[...]
    columns = [
        jnp.any(lists == v * NB + b, axis=1, keepdims=True).astype(F32) for b in range(NB)
    ]
    member = jnp.concatenate(columns, axis=1)
    langs = lists.shape[0]
    hit = (lax.broadcasted_iota(jnp.int32, (langs, TOK), 0) == lane_ref[0:1, :]).astype(F32)
    allowed[...] = lax.dot_general(
        member, hit, (((0,), (0,)), ((), ())), preferred_element_type=F32
    )

    trade.wait_recv()
    kept = jnp.where(c == 0, low, high)
    first = jnp.where(c == 0, kept, swap[1])
    second = jnp.where(c == 0, swap[1], kept)

    def spot(px, pz, n=16):
        row = pl.multiple_of((px * NZ + pz) * 16, 16)
        return tokens.at[pl.ds(row, n), pl.ds(pl.multiple_of(c * HALF, HALF), HALF)]

    own_row = pl.multiple_of((x * NZ + z) * 16, 16)
    tokens[pl.ds(own_row, 16), pl.ds(pl.multiple_of(c * HALF, HALF), HALF)] = (
        jnp.concatenate([first, second], axis=0).astype(BF16)
    )

    def z_send(origin, step):
        block = spot(x, lax.rem(z + origin + 2 * NZ, NZ))
        remote(block, block, sem_z_send, sem_z.at[origin - step + NZ], at_z(step)).start()

    def x_wait(j, k):
        block = spot(lax.rem(x + XPEERS[j], NX), lax.rem(z + k + 2 * NZ, NZ))
        remote(block, block, sem_x_send.at[j], sem_x.at[j, k + NZ], partner).wait_recv()
        remote(block, block, sem_c_send.at[j], sem_c.at[j], partner).start()

    for k in range(1, REACH + 1):
        z_send(0, k)
        z_send(0, -k)
    lag = 4
    for n, k in enumerate(ZORDER):
        block = spot(x, lax.rem(z + k + 2 * NZ, NZ))
        if k:
            remote(block, block, sem_z_send, sem_z.at[k + NZ], partner).wait_recv()
        if k == -REACH:
            for step in range(1, NZ // 2 - REACH + 1):
                z_send(k, step)
        if k == REACH:
            for step in range(1, NZ // 2 - REACH):
                z_send(k, -step)
        for j, xk in enumerate(XPEERS):
            seen = XPEERS.index(NX - xk)
            remote(
                block, block, sem_x_send.at[j], sem_x.at[seen, k + NZ], at_x(xk)
            ).start()
        remote(block, block, sem_c_send.at[3], sem_c.at[3], partner).start()
        if n >= lag:
            for j in range(3):
                x_wait(j, ZORDER[n - lag])
    for k in ZORDER[NZ - lag:]:
        for j in range(3):
            x_wait(j, k)

    load.wait()
    log_counts = jnp.log(counts_ref[...].astype(F32))
    word = v * ROWS + lax.broadcasted_iota(jnp.int32, (BLK, CHUNK), 0)

    for j, xk in ((3, 0), (0, XPEERS[0]), (1, XPEERS[1]), (2, XPEERS[2])):
        px = lax.rem(x + xk, NX)
        whole = spot(px, 0, CHUNK)
        remote(whole, whole, sem_c_send.at[j], sem_c.at[j], partner).wait_recv()
        lane = pl.multiple_of(px * CHUNK, CHUNK)
        held = tokens[pl.ds(lane, CHUNK), :]
        target = lane_ref[1:2, pl.ds(lane, CHUNK)]
        top = jnp.full((1, CHUNK), FILL, F32)
        hit_logit = jnp.zeros((1, CHUNK), F32)
        for b in range(NB):
            score = lax.dot_general(
                table[b * BLK:(b + 1) * BLK, :], held, (((1,), (1,)), ((), ())),
                preferred_element_type=F32,
            ) - log_counts[0:1, b:b + 1]
            score = jnp.where(allowed[b:b + 1, pl.ds(lane, CHUNK)] > 0.5, score, FILL)
            logits[b * BLK:(b + 1) * BLK, pl.ds(lane, CHUNK)] = score
            top = jnp.maximum(top, jnp.max(score, axis=0, keepdims=True))
            hit_logit += jnp.sum(
                jnp.where(word + b * BLK == target, score, 0.0), axis=0, keepdims=True
            )
        total = jnp.zeros((1, CHUNK), F32)
        for b in range(NB):
            share = jnp.exp(logits[b * BLK:(b + 1) * BLK, pl.ds(lane, CHUNK)] - top)
            logits[b * BLK:(b + 1) * BLK, pl.ds(lane, CHUNK)] = share
            total += jnp.sum(share, axis=0, keepdims=True)
        peak_row[0:1, pl.ds(lane, CHUNK)] = top
        local = top + jnp.log(total)
        for r in range(CHUNK // 128):
            row = px * (CHUNK // 128) + r
            lse_out[row] = local[:, r * 128:(r + 1) * 128]
            tgt_out[row] = hit_logit[:, r * 128:(r + 1) * 128]

    slot = x * 2 + c
    for i, (k, f) in enumerate(xc_peers):
        remote(lse_out, s1.at[slot], sem_s1s.at[i], sem_s1.at[slot], at_x(k, f)).start()

    def slot_of(k, f):
        return lax.rem(x + k, NX) * 2 + ((1 - c) if f else c)

    parts = [lse_out[...]]
    for i, (k, f) in enumerate(xc_peers):
        there = slot_of(k, f)
        remote(lse_out, s1.at[there], sem_s1s.at[i], sem_s1.at[there], partner).wait_recv()
        parts.append(s1[there])
    l1 = merge(parts)
    l1_out[...] = l1
    z_far_first = sorted(range(1, NZ), key=lambda k: -min(k, NZ - k))
    for k in z_far_first:
        remote(l1_out, s2.at[z], sem_s2s.at[k], sem_s2.at[z], at_z(k)).start()
    for i, (k, f) in enumerate(xc_peers):
        remote(tgt_out, t1.at[slot], sem_t1s.at[i], sem_t1.at[slot], at_x(k, f)).start()
    tsum = tgt_out[...]
    for i, (k, f) in enumerate(xc_peers):
        there = slot_of(k, f)
        remote(tgt_out, t1.at[there], sem_t1s.at[i], sem_t1.at[there], partner).wait_recv()
        tsum = tsum + t1[there]
    tsum_out[...] = tsum
    for k in range(1, NZ):
        far = lax.rem(z + k, NZ)
        row = x * 2 + lax.div(far, 8)
        remote(
            tsum_out.at[row], t2.at[z], sem_t2s.at[k], sem_t2.at[z], at_z(k)
        ).start()

    parts = [l1]
    for k in range(1, NZ):
        there = lax.rem(z + k, NZ)
        remote(l1_out, s2.at[there], sem_s2s.at[k], sem_s2.at[there], partner).wait_recv()
        parts.append(s2[there])
    log_total = merge(parts)
    l1_out_row = x * 2 + lax.div(z, 8)
    for r in range(TOK // 128):
        total_row[0:1, r * 128:(r + 1) * 128] = log_total[r]

    scale = jnp.exp(peak_row[0:1, :] - total_row[0:1, :])
    word = v * ROWS + lax.broadcasted_iota(jnp.int32, (QROWS, TOK), 0)

    def quarter(q):
        row = pl.multiple_of(q * QROWS, QROWS)
        weights = logits[pl.ds(row, QROWS), :] * scale
        weights = weights - (word + row == lane_ref[1:2, :]).astype(F32)
        probs[...] = weights.astype(BF16)
        return lax.dot_general(
            probs[...], tokens[...], (((1,), (0,)), ((), ())), preferred_element_type=F32
        )

    for i, k in enumerate((2, 1, 3)):
        py = lax.rem(y + k, NY)
        send_buf[i] = quarter(py).astype(BF16)
        seen = (2, 1, 3).index(NY - k)
        remote(
            send_buf.at[i], recv_buf.at[seen], sem_rs.at[i], sem_rr.at[seen],
            dev(x, z, c, py),
        ).start()
    own = quarter(y)

    tgt = tsum_out[l1_out_row]
    for k in range(1, NZ):
        there = lax.rem(z + k, NZ)
        remote(
            tsum_out.at[0], t2.at[there], sem_t2s.at[k], sem_t2.at[there], partner
        ).wait_recv()
        tgt = tgt + t2[there]
    lane0 = lax.rem(z, 8) * 16 + c * 8
    lse_row = total_row[0:1, pl.ds(pl.multiple_of(l1_out_row * 128, 128), 128)]
    loss = jnp.broadcast_to(lse_row - tgt, (8, 128))
    loss_ref[...] = pltpu.roll(loss, lax.rem(128 - lane0, 128), 1)

    for i in (1, 2, 0):
        remote(
            send_buf.at[i], recv_buf.at[i], sem_rs.at[i], sem_rr.at[i], partner
        ).wait_recv()
        own = own + recv_buf[i].astype(F32)
    out_buf[...] = own.astype(BF16)
    put = pltpu.make_async_copy(out_buf, grad_ref, sem_out)
    put.start()

    trade.wait_send()
    remote(
        tokens.at[pl.ds(0, 240), pl.ds(0, HALF)], tokens.at[pl.ds(0, 240), pl.ds(0, HALF)],
        sem_z_send, sem_z.at[0], partner,
    ).wait_send()
    whole = tokens.at[pl.ds(0, CHUNK), pl.ds(0, HALF)]
    for j in range(3):
        remote(whole, whole, sem_x_send.at[j], sem_x.at[j, 0], partner).wait_send()
    for j in range(4):
        remote(whole, whole, sem_c_send.at[j], sem_c.at[j], partner).wait_send()
    for i in range(7):
        remote(lse_out, s1.at[0], sem_s1s.at[i], sem_s1.at[0], partner).wait_send()
        remote(tgt_out, t1.at[0], sem_t1s.at[i], sem_t1.at[0], partner).wait_send()
    for k in range(1, NZ):
        remote(l1_out, s2.at[0], sem_s2s.at[k], sem_s2.at[0], partner).wait_send()
        remote(tsum_out.at[0], t2.at[0], sem_t2s.at[k], sem_t2.at[0], partner).wait_send()
    for i in range(3):
        remote(send_buf.at[i], recv_buf.at[i], sem_rs.at[i], sem_rr.at[i], partner).wait_send()
    put.wait()


def body(hidden, embedding, block_counts, lang_blocks, sent_lang, targets):
    v, y = lax.axis_index("vocab"), lax.axis_index("batch")
    lang_lane = jnp.broadcast_to(sent_lang[:, None], (64, 16)).reshape(1, TOK)
    plane = lax.dynamic_index_in_dim(targets.reshape(128, NY, 8), y, 1, keepdims=False)
    lanes = jnp.concatenate(
        [lang_lane, plane.reshape(1, TOK), jnp.zeros((6, TOK), jnp.int32)], axis=0
    )
    vmem, dma = pltpu.VMEM, pltpu.SemaphoreType.DMA
    spec = pl.BlockSpec(memory_space=pltpu.VMEM)
    loss, grad = pl.pallas_call(
        kernel,
        out_shape=(
            jax.ShapeDtypeStruct((8, 128), F32),
            jax.ShapeDtypeStruct((QROWS, D), BF16),
        ),
        in_specs=[spec, pl.BlockSpec(memory_space=pl.ANY), spec, spec, spec],
        out_specs=(spec, pl.BlockSpec(memory_space=pl.ANY)),
        scratch_shapes=[
            vmem((ROWS, D), BF16),
            vmem((TOK, D), BF16),
            vmem((ROWS, TOK), F32),
            vmem((QROWS, TOK), BF16),
            vmem((2, 8, HALF), F32),
            vmem((NB, TOK), F32),
            vmem((8, TOK), F32),
            vmem((8, TOK), F32),
            vmem((8, 8, 1, 128), F32),
            vmem((NZ, 8, 1, 128), F32),
            vmem((8, 8, 1, 128), F32),
            vmem((NZ, 1, 128), F32),
            vmem((8, 1, 128), F32),
            vmem((8, 1, 128), F32),
            vmem((8, 1, 128), F32),
            vmem((8, 1, 128), F32),
            vmem((3, QROWS, D), BF16),
            vmem((3, QROWS, D), BF16),
            vmem((QROWS, D), BF16),
            dma, dma((2,)), dma, dma((2 * NZ,)), dma((3,)), dma((3, 2 * NZ)),
            dma((4,)), dma((4,)), dma((7,)), dma((8,)), dma((NZ,)), dma((NZ,)),
            dma((7,)), dma((8,)), dma((NZ,)), dma((NZ,)), dma((3,)), dma((3,)), dma,
        ],
        compiler_params=pltpu.CompilerParams(
            collective_id=0, has_side_effects=True, vmem_limit_bytes=48 << 20
        ),
    )(hidden, embedding, block_counts.reshape(1, NB), lang_blocks, lanes)
    return loss[0, :8], grad


def solution(mesh):
    in_specs = (P(("vocab", "batch"), None), P("vocab", None), P("vocab"), P(), P(), P())
    out_specs = (P(("vocab", "batch")), P(("vocab", "batch"), None))
    return jax.shard_map(body, mesh=mesh, in_specs=in_specs, out_specs=out_specs, check_vma=False)
```

time: 707 us -> 89.8 us (0.13)
  blocking collectives: 501 us -> 0 us
  waiting for transfers between devices: 171 us -> 0 us
  Pallas kernels: 0 us -> 81.3 us
  between operations: 14.2 us -> 0.67 us
  matrix products: 9.95 us -> 0 us
  other arithmetic: 9.04 us -> 0.07 us
    psum x1 -> x0, blocking collectives: 254 us -> none  [body(): denominator, target_logit = lax.psum((local_total, local_target), 'vocab')]
    pmax x1 -> x0, blocking collectives: 246 us -> none  [body(): peak_value = lax.pmax(local_peak, 'vocab')]
    all_gather x1 -> x0, waiting for transfers between devices: 144 us -> none  [body(): gathered = lax.all_gather(hidden, 'vocab', axis=0, tiled=True)]
    pallas_call x0 -> x1, Pallas kernels: none -> 81.3 us  [body(): pl.pallas_call(kernel, out_shape=(jax.ShapeDtypeStruct((8, 128), F32), ja...]
    reduce_scatter x1 -> x0, waiting for transfers between devices: 25.6 us -> none  [body(): lax.psum_scatter(rounded_terms, 'batch', scatter_dimension=0, tiled=True)]
    dot_general x3 -> x0, matrix products: 9.95 us -> none  [the longest x1 5.89 us: body(): lax.dot_general(gathered, embedding, (((1,), (1,)), ((), ())), preferred_...]
  transfers between devices with their start and end apart: 2 -> 0, of which waited for: 2 -> 0; matrix products, arithmetic and copies ran while one was open for 1% -> 0% of each run, Pallas kernels for 0% -> 0%
where the time goes in v1:
time: 89.8 us; the launch traced here: 89.5 us
  Pallas kernels  81.3 us (91%)
  local copies, waits for them, and re-layouts  7.46 us (8%)
    pallas_call x1, Pallas kernels, body(): pl.pallas_call(kernel, out_shape=(jax.ShapeDtypeStruct((8, 128), F32), ja...  81.3 us
    unnamed x8, local copies, waits for them, and re-layouts  4.7 us

profile of v1, /device:TPU:1, one launch (start us, length us, event | category | flops | bytes accessed | tf_op | source)
XLA Modules:
  0.0 89.5 jit_solution(14789451674116426455)
XLA Ops:
  0.6 0.1 pad.2.clone
  0.7 0.7 broadcast_in_dim.4
  1.4 0.1 reshape.19
  1.5 0.9 %copy.9.lists_ref = s32[200,64]{1,0:T(8,128)S(1)} copy(s32[200,64]{0,1:T(8,128)} %param.9) | data formatting | bytes 102400 | tf_op args[3]
  2.5 1.1 %reshape.20 = s32[128,4,8]{2,1,0:T(4,128)S(1)} reshape(s32[4096]{0:T(1024)} %param.11) | data formatting | bytes 32768 | tf_op jit(solution)/shard_map/reshape | solution.py:289
  3.5 0.2 dynamic-slice_reduce_fusion
  3.7 0.1 reshape.21
  3.8 0.1 add_add_fusion.lane_ref
  3.9 0.0 copy-start
  3.9 1.6 %copy-done = bf16[1024,1024]{1,0:T(8,128)(2,1)S(1)} copy-done((bf16[1024,1024]{1,0:T(8,128)(2,1)S(1)}, bf16[1024,1024]{1,0:T(8,128)(2,1)}, u32[]{:S(2)}) %copy-start) | copy-done | bytes 2097176
  5.5 0.0 copy-start.1
  5.5 0.7 copy-done.1
  6.2 0.0 copy-start.2
  6.2 0.7 copy-done.2
  6.9 81.3 %shard_map.77 = (f32[8,128]{1,0:T(8,128)S(1)}, bf16[256,1024]{1,0:T(8,128)(2,1)S(1)}) custom-call(bf16[8,1024]{1,0:T(8,128)(2,1)S(1)} %copy-done.1, bf16[1024,1024]{1,0:T(8,128)(2,1)S(1)} %copy-done, s32[1,8]{1,0:T(1,128)S(1)} %bitcast.3, s32[200,64]{1,0:T(8,128)S(1)} %copy.9.lists_ref, s32[8,1024]{1,0:T(8,128)S(1)} %add_add_fusion.lane_ref), custom_call_target="tpu_custom_call" | custom-call | tf_op jit(solution)/shard_map/pallas_call | solution.py:295
  88.2 0.5 slice_bitcast_fusion
  88.7 0.8 copy.11
  (1 shorter events, 0.0 us)
Async XLA Ops:
  3.9 1.6 %copy-start = (bf16[1024,1024]{1,0:T(8,128)(2,1)S(1)}, bf16[1024,1024]{1,0:T(8,128)(2,1)}, u32[]{:S(2)}) copy-start(bf16[1024,1024]{1,0:T(8,128)(2,1)} %emb_ref.1) | copy-start | bytes 6291460
  5.5 0.7 copy-start.1
  6.2 0.7 copy-start.2

commit v2 on v1

v2 whole, which is shorter than its diff:
```python
import functools

import jax
import jax.numpy as jnp
from jax import lax
from jax.experimental import pallas as pl
from jax.experimental.pallas import tpu as pltpu
from jax.sharding import PartitionSpec as P

MESH = pl.DeviceIdType.MESH
F32, BF16, I32 = jnp.float32, jnp.bfloat16, jnp.int32
NX, NZ, NY = 4, 16, 4
D = 1024
HALF = 512
ROWS = 1024
TOK = 1024
NB = 8
BLK = 128
QROWS = 256
CHUNK = 256
FILL = -3e38
REACH = 4
ZORDER = [0] + [s * k for k in range(1, 8) for s in (1, -1)] + [-8]
XPEERS = (1, 3, 2)
XC_PEERS = [(k, f) for f in (0, 1) for k in range(NX) if (k, f) != (0, 0)]
CHUNKS = (0, 3, 1, 2)


def remote(src, dst, send, recv, device):
    return pltpu.make_async_remote_copy(
        src_ref=src, dst_ref=dst, send_sem=send, recv_sem=recv,
        device_id=device, device_id_type=MESH,
    )


def merge(parts):
    top = functools.reduce(jnp.maximum, parts)
    total = functools.reduce(jnp.add, [jnp.exp(p - top) for p in parts])
    return top + jnp.log(total)


def dot(a, b, contract):
    return lax.dot_general(a, b, (contract, ((), ())), preferred_element_type=F32)


def kernel(
    hid_hbm, emb_hbm, counts_hbm, lists_hbm, sent_hbm, targets_hbm,
    loss_ref, grad_ref,
    hid, table, counts, lists, sent, targets,
    tokens, tokens2, logits, logits2, probs, sums, swap, allowed, rows,
    s1, s2, t1, t2, lse_out, l1_out, tgt_out, tsum_out, l_out, l_in,
    send_buf, recv_buf, out_buf,
    sem_load, sem_swap, sem_z_send, sem_z, sem_x_send, sem_x, sem_c_send, sem_c,
    sem_y_send, sem_y, sem_c2_send, sem_c2,
    sem_s1s, sem_s1, sem_s2s, sem_s2, sem_t1s, sem_t1, sem_t2s, sem_t2,
    sem_l, sem_rs, sem_rr, sem_out,
):
    v, y = lax.axis_index("vocab"), lax.axis_index("batch")
    c = lax.rem(v, 2)
    z = lax.rem(lax.div(v, 2), NZ)
    x = lax.div(v, 2 * NZ)

    def dev(px, pz, pc, py):
        return {"vocab": (px * NZ + pz) * 2 + pc, "batch": py}

    def at_z(k):
        return dev(x, lax.rem(z + k + 2 * NZ, NZ), c, y)

    def at_x(k, flip=0):
        return dev(lax.rem(x + k, NX), z, (1 - c) if flip else c, y)

    def at_y(k):
        return dev(x, z, c, lax.rem(y + k, NY))

    partner = dev(x, z, 1 - c, y)
    across = at_y(2)

    pairs = (
        (hid_hbm, hid), (lists_hbm, lists), (sent_hbm, sent), (targets_hbm, targets),
        (counts_hbm, counts), (emb_hbm, table),
    )
    loads = [
        pltpu.make_async_copy(src, dst, sem_load.at[i]) for i, (src, dst) in enumerate(pairs)
    ]
    for load in loads:
        load.start()

    barrier = pltpu.get_barrier_semaphore()
    near = [at_x(k, f) for k, f in XC_PEERS]
    near += [at_z(s * k) for k in range(1, REACH + 1) for s in (1, -1)]
    near += [at_y(k) for k in range(1, NY)]
    for peer in near:
        pl.semaphore_signal(barrier, inc=1, device_id=peer, device_id_type=MESH)

    for load in loads[:4]:
        load.wait()
    lane = lax.broadcasted_iota(I32, (1, TOK), 1)
    lane_x, lane_z = (lane >> 4) & 3, (z + (lane >> 6)) & (NZ - 1)
    place = ((lane_z & 1) << 6) + (((lane >> 3) & 1) << 5) + (lane & 7)
    ids = targets[...]
    digits = jnp.concatenate([ids & 255, (ids >> 8) & 255, ids >> 16], axis=0).astype(F32).astype(BF16)
    here = lax.broadcasted_iota(I32, (32, TOK), 0) == lane_x * 8 + (lane_z >> 1)

    def plane_targets(py):
        pick = lax.broadcasted_iota(I32, (128, TOK), 0) == place + py * 8
        found = dot(digits, pick.astype(F32).astype(BF16), ((1,), (0,)))
        value = found[:32] + found[32:64] * 256.0 + found[64:] * 65536.0
        return jnp.sum(jnp.where(here, value, 0.0), axis=0, keepdims=True).astype(I32)

    own_targets = plane_targets(y)
    other_targets = plane_targets(lax.rem(y + 2, NY))
    sentence = lax.broadcasted_iota(I32, (64, TOK), 0) == lane_x * NZ + lane_z
    lang = dot(
        jnp.broadcast_to(sent[...], (8, 64)).astype(F32).astype(BF16),
        sentence.astype(F32).astype(BF16), ((1,), (0,)),
    )[0:1].astype(I32)
    lists_now = lists[...]
    member = jnp.concatenate(
        [jnp.any(lists_now == v * NB + b, axis=1, keepdims=True).astype(F32) for b in range(NB)],
        axis=1,
    )
    hit = (lax.broadcasted_iota(I32, (lists.shape[0], TOK), 0) == lang).astype(F32)
    allowed[...] = dot(member, hit, ((0,), (0,)))
    rows[0:1, :] = own_targets
    rows[1:2, :] = other_targets

    mine = hid[...].astype(F32)
    low, high = mine[:, :HALF], mine[:, HALF:]
    swap[0] = jnp.where(c == 0, high, low)
    kept = jnp.where(c == 0, low, high)
    pl.semaphore_wait(barrier, len(near))
    trade = remote(swap.at[0], swap.at[1], sem_swap.at[0], sem_swap.at[1], partner)
    trade.start()
    trade.wait_recv()
    first = jnp.where(c == 0, kept, swap[1])
    second = jnp.where(c == 0, swap[1], kept)

    half = pl.ds(pl.multiple_of(c * HALF, HALF), HALF)

    def spot(ref, slot, px):
        return ref.at[pl.ds(pl.multiple_of((slot % NZ) * 64 + px * 16, 16), 16), half]

    def chunk_of(ref, g):
        return ref.at[pl.ds(g * CHUNK, CHUNK), half]

    tokens[pl.ds(pl.multiple_of(x * 16, 16), 16), half] = (
        jnp.concatenate([first, second], axis=0).astype(BF16)
    )

    def z_send(k, step):
        remote(
            spot(tokens, k, x), spot(tokens, k - step, x),
            sem_z_send, sem_z.at[(k - step) % NZ], at_z(step),
        ).start()

    def share(k, px):
        slot = k % NZ
        g = slot // 4
        block = spot(tokens, slot, px)
        remote(block, block, sem_c_send.at[g], sem_c.at[g], partner).start()
        remote(block, spot(tokens2, slot, px), sem_y_send.at[g], sem_y.at[g], across).start()

    def z_step(k):
        slot = k % NZ
        block = spot(tokens, slot, x)
        if k:
            remote(block, block, sem_z_send, sem_z.at[slot], partner).wait_recv()
        if k == -REACH:
            for step in range(1, NZ // 2 - REACH + 1):
                z_send(k, step)
        if k == REACH:
            for step in range(1, NZ // 2 - REACH):
                z_send(k, -step)
        for j, xk in enumerate(XPEERS):
            seen = XPEERS.index(NX - xk)
            remote(block, block, sem_x_send.at[j], sem_x.at[seen, slot], at_x(xk)).start()
        share(k, x)

    def x_steps(g):
        for slot in range(4 * g, 4 * g + 4) if g < 2 else range(4 * g + 3, 4 * g - 1, -1):
            for j, xk in enumerate(XPEERS):
                px = lax.rem(x + xk, NX)
                block = spot(tokens, slot, px)
                remote(block, block, sem_x_send.at[j], sem_x.at[j, slot], partner).wait_recv()
                share(slot, px)

    def rows_of(g):
        return slice(g * CHUNK, (g + 1) * CHUNK)

    word = lax.broadcasted_iota(I32, (BLK, CHUNK), 0)

    def chunk_logits(g):
        whole = chunk_of(tokens, g)
        remote(whole, whole, sem_c_send.at[g], sem_c.at[g], partner).wait_recv()
        at = rows_of(g)
        held = tokens[at, :]
        target = rows[0:1, at] - v * ROWS
        top = jnp.full((1, CHUNK), FILL, F32)
        hit_logit = jnp.zeros((1, CHUNK), F32)
        for b in range(NB):
            score = dot(table[b * BLK:(b + 1) * BLK, :], held, ((1,), (1,))) - log_counts[0:1, b:b + 1]
            score = jnp.where(allowed[b:b + 1, at] > 0.5, score, FILL)
            logits[b * BLK:(b + 1) * BLK, at] = score
            top = jnp.maximum(top, jnp.max(score, axis=0, keepdims=True))
            hit_logit += jnp.sum(jnp.where(word + b * BLK == target, score, 0.0), axis=0, keepdims=True)
        total = jnp.zeros((1, CHUNK), F32)
        for b in range(NB):
            weight = jnp.exp(logits[b * BLK:(b + 1) * BLK, at] - top)
            logits[b * BLK:(b + 1) * BLK, at] = weight
            total += jnp.sum(weight, axis=0, keepdims=True)
        peaks[g] = top
        local = top + jnp.log(total)
        for r in range(2):
            lse_out[2 * g + r] = local[:, r * 128:(r + 1) * 128]
            tgt_out[2 * g + r] = hit_logit[:, r * 128:(r + 1) * 128]
        for i, (k, f) in enumerate(XC_PEERS):
            remote(
                lse_out.at[pl.ds(2 * g, 2)], s1.at[my_slot, pl.ds(2 * g, 2)],
                sem_s1s.at[g, i], sem_s1.at[g, my_slot], at_x(k, f),
            ).start()

    my_slot = x * 2 + c

    def slot_of(k, f):
        return lax.rem(x + k, NX) * 2 + ((1 - c) if f else c)

    far_first = sorted(range(1, NZ), key=lambda k: -min(k, NZ - k))

    def chunk_totals(g):
        two = pl.ds(2 * g, 2)
        parts = [lse_out[two]]
        for i, (k, f) in enumerate(XC_PEERS):
            there = slot_of(k, f)
            remote(
                lse_out.at[two], s1.at[there, two], sem_s1s.at[g, i], sem_s1.at[g, there], partner
            ).wait_recv()
            parts.append(s1[there, two])
        l1_out[two] = merge(parts)
        for k in far_first:
            remote(
                l1_out.at[two], s2.at[z, two], sem_s2s.at[g, k], sem_s2.at[g, z], at_z(k)
            ).start()

    peaks = [None] * 4

    for k in range(REACH, 0, -1):
        z_send(0, k)
        z_send(0, -k)
    for k in ZORDER:
        z_step(k)
    loads[4].wait()
    loads[5].wait()
    log_counts = jnp.log(counts[...].astype(F32))

    ca, cb, cc, cd = CHUNKS
    x_steps(ca)
    x_steps(cb)
    chunk_logits(ca)
    x_steps(cc)
    chunk_logits(cb)
    chunk_totals(ca)
    x_steps(cd)
    chunk_logits(cc)
    chunk_totals(cb)
    chunk_logits(cd)
    chunk_totals(cc)
    chunk_totals(cd)

    for i, (k, f) in enumerate(XC_PEERS):
        remote(tgt_out, t1.at[my_slot], sem_t1s.at[i], sem_t1.at[my_slot], at_x(k, f)).start()

    up = lax.rem(y + 1, NY) * 2
    down = lax.rem(y + 3, NY) * 2 + 1
    held_blocks = (up, down, y * 2, y * 2 + 1)
    peaks2 = [None] * 4

    def pass_on(g):
        whole = chunk_of(tokens2, g)
        remote(whole, whole, sem_y_send.at[g], sem_y.at[g], partner).wait_recv()
        remote(whole, whole, sem_c2_send.at[g], sem_c2.at[g], partner).start()

    block_lane = lax.broadcasted_iota(I32, (1, NB), 1)
    block_row = lax.broadcasted_iota(I32, (NB, CHUNK), 0)

    def other_logits(g):
        whole = chunk_of(tokens2, g)
        remote(whole, whole, sem_c2_send.at[g], sem_c2.at[g], partner).wait_recv()
        at = rows_of(g)
        held = tokens2[at, :]
        may = allowed[:, at]
        top = jnp.full((1, CHUNK), FILL, F32)
        for i, b in enumerate(held_blocks):
            entry = table[pl.ds(pl.multiple_of(b * BLK, BLK), BLK), :]
            less = jnp.sum(jnp.where(block_lane == b, log_counts, 0.0), axis=1, keepdims=True)
            ok = jnp.sum(jnp.where(block_row == b, may, 0.0), axis=0, keepdims=True) > 0.5
            score = jnp.where(ok, dot(entry, held, ((1,), (1,))) - less, FILL)
            logits2[i * BLK:(i + 1) * BLK, at] = score
            top = jnp.maximum(top, jnp.max(score, axis=0, keepdims=True))
        for i in range(4):
            logits2[i * BLK:(i + 1) * BLK, at] = jnp.exp(logits2[i * BLK:(i + 1) * BLK, at] - top)
        peaks2[g] = top

    pass_on(ca)
    pass_on(cb)
    other_logits(ca)
    pass_on(cc)
    other_logits(cb)
    pass_on(cd)
    other_logits(cc)

    first_half = lax.broadcasted_iota(I32, (1, 128), 1) < 64
    parts = [[l1_out[r]] for r in range(8)]
    for k in far_first[::-1]:
        there = lax.rem(z + k, NZ)
        for g in CHUNKS:
            two = pl.ds(2 * g, 2)
            remote(
                l1_out.at[two], s2.at[there, two], sem_s2s.at[g, k], sem_s2.at[g, there], partner
            ).wait_recv()
        theirs = [s2[there, r] for r in range(8)]
        if k % 2:
            turned = [pltpu.roll(t, 64, 1) for t in theirs]
        for r in range(8):
            if k % 2:
                before = ((2 * r - k - 1) // 2) % 8
                parts[r].append(jnp.where(first_half, turned[before], turned[(before + 1) % 8]))
            else:
                parts[r].append(theirs[(r - k // 2) % 8])
    total_rows = [merge(p) for p in parts]
    for r in range(8):
        l_out[r] = total_rows[r]
    tell = remote(l_out, l_in, sem_l.at[0], sem_l.at[1], across)
    tell.start()
    other_logits(cd)

    scale = jnp.exp(jnp.concatenate(peaks, axis=1) - jnp.concatenate(total_rows, axis=1))
    deep = lax.broadcasted_iota(I32, (BLK, TOK), 0)
    own_row = rows[0:1, :] - v * ROWS
    other_row = rows[1:2, :] - v * ROWS

    def fill_probs(source, at, b, n, factor, target):
        weight = source[pl.ds(pl.multiple_of(at * BLK, BLK), BLK), :] * factor
        weight = weight - (deep + b * BLK == target).astype(F32)
        probs[n * BLK:(n + 1) * BLK, :] = weight.astype(BF16)

    for n, b in enumerate(held_blocks):
        fill_probs(logits, b, b, n, scale, own_row)
    sums[...] = dot(probs[...], tokens[...], ((1,), (0,)))

    tell.wait_recv()
    other_total = jnp.concatenate([l_in[r] for r in range(8)], axis=1)
    scale2 = jnp.exp(jnp.concatenate(peaks2, axis=1) - other_total)
    for n, b in enumerate(held_blocks):
        fill_probs(logits2, n, b, n, scale2, other_row)
    for n, to in ((0, at_y(1)), (1, at_y(3))):
        at = slice(n * BLK, (n + 1) * BLK)
        send_buf[n] = (sums[at, :] + dot(probs[at, :], tokens2[...], ((1,), (0,)))).astype(BF16)
        remote(send_buf.at[n], recv_buf.at[n], sem_rs.at[n], sem_rr.at[n], to).start()

    tsum = tgt_out[...]
    for i, (k, f) in enumerate(XC_PEERS):
        there = slot_of(k, f)
        remote(tgt_out, t1.at[there], sem_t1s.at[i], sem_t1.at[there], partner).wait_recv()
        tsum = tsum + t1[there]
    tsum_out[...] = tsum
    for k in far_first:
        remote(tsum_out.at[k // 2], t2.at[z], sem_t2s.at[k], sem_t2.at[z], at_z(k)).start()

    sums[2 * BLK:, :] += dot(probs[2 * BLK:, :], tokens2[...], ((1,), (0,)))

    tgt = tsum_out[0]
    for k in far_first[::-1]:
        there = lax.rem(z + k, NZ)
        remote(tsum_out.at[0], t2.at[there], sem_t2s.at[k], sem_t2.at[there], partner).wait_recv()
        theirs = t2[there]
        tgt = tgt + (pltpu.roll(theirs, 64, 1) if k % 2 else theirs)
    lane0 = x * 16 + c * 8
    loss = jnp.broadcast_to(l_out[0] - tgt, (8, 128))
    loss_ref[...] = pltpu.roll(loss, lax.rem(128 - lane0, 128), 1)

    for n in range(2):
        remote(send_buf.at[n], recv_buf.at[n], sem_rs.at[n], sem_rr.at[n], partner).wait_recv()
        at = slice(n * BLK, (n + 1) * BLK)
        out_buf[at, :] = (sums[(2 + n) * BLK:(3 + n) * BLK, :] + recv_buf[n].astype(F32)).astype(BF16)
    put = pltpu.make_async_copy(out_buf, grad_ref, sem_out)
    put.start()

    trade.wait_send()
    tell.wait_send()
    block = tokens.at[pl.ds(0, 240), pl.ds(0, HALF)]
    remote(block, block, sem_z_send, sem_z.at[0], partner).wait_send()
    whole = chunk_of(tokens, 0)
    for j in range(3):
        remote(whole, whole, sem_x_send.at[j], sem_x.at[j, 0], partner).wait_send()
    for g in range(4):
        remote(whole, whole, sem_c_send.at[g], sem_c.at[g], partner).wait_send()
        remote(whole, whole, sem_y_send.at[g], sem_y.at[g], partner).wait_send()
        remote(whole, whole, sem_c2_send.at[g], sem_c2.at[g], partner).wait_send()
        two = pl.ds(0, 2)
        for i in range(7):
            remote(lse_out.at[two], s1.at[0, two], sem_s1s.at[g, i], sem_s1.at[g, 0], partner).wait_send()
        for k in range(1, NZ):
            remote(l1_out.at[two], s2.at[0, two], sem_s2s.at[g, k], sem_s2.at[g, 0], partner).wait_send()
    for i in range(7):
        remote(tgt_out, t1.at[0], sem_t1s.at[i], sem_t1.at[0], partner).wait_send()
    for k in range(1, NZ):
        remote(tsum_out.at[0], t2.at[0], sem_t2s.at[k], sem_t2.at[0], partner).wait_send()
    for n in range(2):
        remote(send_buf.at[n], recv_buf.at[n], sem_rs.at[n], sem_rr.at[n], partner).wait_send()
    put.wait()


def body(hidden, embedding, block_counts, lang_blocks, sent_lang, targets):
    vmem, dma = pltpu.VMEM, pltpu.SemaphoreType.DMA
    anywhere = pl.BlockSpec(memory_space=pl.ANY)
    loss, grad = pl.pallas_call(
        kernel,
        out_shape=(
            jax.ShapeDtypeStruct((8, 128), F32),
            jax.ShapeDtypeStruct((QROWS, D), BF16),
        ),
        in_specs=[anywhere] * 6,
        out_specs=(pl.BlockSpec(memory_space=pltpu.VMEM), anywhere),
        scratch_shapes=[
            vmem(hidden.shape, BF16),
            vmem((ROWS, D), BF16),
            vmem((1, NB), I32),
            vmem(lang_blocks.shape, I32),
            vmem((1, 64), I32),
            vmem((32, 128), I32),
            vmem((TOK, D), BF16),
            vmem((TOK, D), BF16),
            vmem((ROWS, TOK), F32),
            vmem((4 * BLK, TOK), F32),
            vmem((4 * BLK, TOK), BF16),
            vmem((4 * BLK, D), F32),
            vmem((2, 8, HALF), F32),
            vmem((NB, TOK), F32),
            vmem((8, TOK), I32),
            vmem((8, 8, 1, 128), F32),
            vmem((NZ, 8, 1, 128), F32),
            vmem((8, 8, 1, 128), F32),
            vmem((NZ, 1, 128), F32),
            vmem((8, 1, 128), F32),
            vmem((8, 1, 128), F32),
            vmem((8, 1, 128), F32),
            vmem((8, 1, 128), F32),
            vmem((8, 1, 128), F32),
            vmem((8, 1, 128), F32),
            vmem((2, BLK, D), BF16),
            vmem((2, BLK, D), BF16),
            vmem((QROWS, D), BF16),
            dma((6,)), dma((2,)), dma, dma((NZ,)), dma((3,)), dma((3, NZ)),
            dma((4,)), dma((4,)), dma((4,)), dma((4,)), dma((4,)), dma((4,)),
            dma((4, 7)), dma((4, 8)), dma((4, NZ)), dma((4, NZ)),
            dma((7,)), dma((8,)), dma((NZ,)), dma((NZ,)),
            dma((2,)), dma((2,)), dma((2,)), dma,
        ],
        compiler_params=pltpu.CompilerParams(
            collective_id=0, has_side_effects=True, vmem_limit_bytes=56 << 20
        ),
    )(
        hidden, embedding, block_counts.reshape(1, NB), lang_blocks,
        sent_lang.reshape(1, 64), targets.reshape(32, 128),
    )
    return loss[0, :8], grad


def solution(mesh):
    in_specs = (P(("vocab", "batch"), None), P("vocab", None), P("vocab"), P(), P(), P())
    out_specs = (P(("vocab", "batch")), P(("vocab", "batch"), None))
    return jax.shard_map(body, mesh=mesh, in_specs=in_specs, out_specs=out_specs, check_vma=False)
```

time: 89.8 us -> 70.8 us (0.79)
  Pallas kernels: 81.3 us -> 64.6 us
  local copies, waits for them, and re-layouts: 7.46 us -> 4.63 us
    pallas_call x1, Pallas kernels: 81.3 us -> 64.6 us  [body(): pl.pallas_call(kernel, out_shape=(jax.ShapeDtypeStruct((8, 128), F32), ja...]
    unnamed x8 -> x2, local copies, waits for them, and re-layouts: 4.7 us -> 3.45 us
    reshape x3 -> x0, local copies, waits for them, and re-layouts: 1.24 us -> none  [the longest x1 1.06 us: body(): targets.reshape(128, NY, 8)]
where the time goes in v2:
time: 70.8 us; the launch traced here: 69.9 us
  Pallas kernels  64.6 us (91%)
  local copies, waits for them, and re-layouts  4.63 us (7%)
    pallas_call x1, Pallas kernels, body(): pl.pallas_call(kernel, out_shape=(jax.ShapeDtypeStruct((8, 128), F32), ja...  64.6 us
    unnamed x2, local copies, waits for them, and re-layouts  3.45 us

profile of v2, /device:TPU:1, one launch (start us, length us, event | category | flops | bytes accessed | tf_op | source)
XLA Modules:
  0.0 69.9 jit_solution(2643174989737241065)
XLA Ops:
  0.6 1.6 %copy.8.lists_hbm = s32[200,64]{1,0:T(8,128)} copy(s32[200,64]{0,1:T(8,128)} %param.9) | data formatting | bytes 102400 | tf_op args[3]
  2.2 64.6 %shard_map.77 = (f32[8,128]{1,0:T(8,128)}, bf16[256,1024]{1,0:T(8,128)(2,1)}) custom-call(bf16[8,1024]{1,0:T(8,128)(2,1)} %hid_hbm.1, bf16[1024,1024]{1,0:T(8,128)(2,1)} %emb_hbm.1, s32[1,8]{1,0:T(1,128)} %bitcast.6, s32[200,64]{1,0:T(8,128)} %copy.8.lists_hbm, s32[1,64]{1,0:T(1,128)} %bitcast.7, s32[32,128]{1,0:T(8,128)} %bitcast.5), custom_call_target="tpu_custom_call" | custom-call | tf_op jit(solution)/shard_map/pallas_call | solution.py:416
  66.8 1.2 %slice_bitcast_fusion = f32[8]{0:T(128)} fusion(f32[8,128]{1,0:T(8,128)} %get-tuple-element.4), kind=kLoop, calls=%fused_computation | loop fusion | bytes 64 | tf_op jit(solution)/shard_map/squeeze | solution.py:466
  68.0 1.9 %copy.10 = bf16[256,1024]{1,0:T(8,128)(2,1)} copy(bf16[256,1024]{1,0:T(8,128)(2,1)} %get-tuple-element.9) | data formatting | bytes 1048576

commit v3 on v2

--- a/solution.py
+++ b/solution.py
@@ -19,7 +19,7 @@
 QROWS = 256
 CHUNK = 256
 FILL = -3e38
-REACH = 4
+REACH = 2
 ZORDER = [0] + [s * k for k in range(1, 8) for s in (1, -1)] + [-8]
 XPEERS = (1, 3, 2)
 XC_PEERS = [(k, f) for f in (0, 1) for k in range(NX) if (k, f) != (0, 0)]
@@ -45,11 +45,11 @@
 
 def kernel(
     hid_hbm, emb_hbm, counts_hbm, lists_hbm, sent_hbm, targets_hbm,
-    loss_ref, grad_ref,
+    loss_ref, own_ref, recv_ref,
     hid, table, counts, lists, sent, targets,
     tokens, tokens2, logits, logits2, probs, sums, swap, allowed, rows,
     s1, s2, t1, t2, lse_out, l1_out, tgt_out, tsum_out, l_out, l_in,
-    send_buf, recv_buf, out_buf,
+    send_buf,
     sem_load, sem_swap, sem_z_send, sem_z, sem_x_send, sem_x, sem_c_send, sem_c,
     sem_y_send, sem_y, sem_c2_send, sem_c2,
     sem_s1s, sem_s1, sem_s2s, sem_s2, sem_t1s, sem_t1, sem_t2s, sem_t2,
@@ -92,38 +92,7 @@
     for peer in near:
         pl.semaphore_signal(barrier, inc=1, device_id=peer, device_id_type=MESH)
 
-    for load in loads[:4]:
-        load.wait()
-    lane = lax.broadcasted_iota(I32, (1, TOK), 1)
-    lane_x, lane_z = (lane >> 4) & 3, (z + (lane >> 6)) & (NZ - 1)
-    place = ((lane_z & 1) << 6) + (((lane >> 3) & 1) << 5) + (lane & 7)
-    ids = targets[...]
-    digits = jnp.concatenate([ids & 255, (ids >> 8) & 255, ids >> 16], axis=0).astype(F32).astype(BF16)
-    here = lax.broadcasted_iota(I32, (32, TOK), 0) == lane_x * 8 + (lane_z >> 1)
-
-    def plane_targets(py):
-        pick = lax.broadcasted_iota(I32, (128, TOK), 0) == place + py * 8
-        found = dot(digits, pick.astype(F32).astype(BF16), ((1,), (0,)))
-        value = found[:32] + found[32:64] * 256.0 + found[64:] * 65536.0
-        return jnp.sum(jnp.where(here, value, 0.0), axis=0, keepdims=True).astype(I32)
-
-    own_targets = plane_targets(y)
-    other_targets = plane_targets(lax.rem(y + 2, NY))
-    sentence = lax.broadcasted_iota(I32, (64, TOK), 0) == lane_x * NZ + lane_z
-    lang = dot(
-        jnp.broadcast_to(sent[...], (8, 64)).astype(F32).astype(BF16),
-        sentence.astype(F32).astype(BF16), ((1,), (0,)),
-    )[0:1].astype(I32)
-    lists_now = lists[...]
-    member = jnp.concatenate(
-        [jnp.any(lists_now == v * NB + b, axis=1, keepdims=True).astype(F32) for b in range(NB)],
-        axis=1,
-    )
-    hit = (lax.broadcasted_iota(I32, (lists.shape[0], TOK), 0) == lang).astype(F32)
-    allowed[...] = dot(member, hit, ((0,), (0,)))
-    rows[0:1, :] = own_targets
-    rows[1:2, :] = other_targets
-
+    loads[0].wait()
     mine = hid[...].astype(F32)
     low, high = mine[:, :HALF], mine[:, HALF:]
     swap[0] = jnp.where(c == 0, high, low)
@@ -165,24 +134,23 @@
         block = spot(tokens, slot, x)
         if k:
             remote(block, block, sem_z_send, sem_z.at[slot], partner).wait_recv()
-        if k == -REACH:
-            for step in range(1, NZ // 2 - REACH + 1):
-                z_send(k, step)
-        if k == REACH:
-            for step in range(1, NZ // 2 - REACH):
-                z_send(k, -step)
+        if k and k % REACH == 0:
+            for step in range(1, REACH + 1):
+                if k < 0 and step - k <= NZ // 2:
+                    z_send(k, step)
+                if k > 0 and step + k < NZ // 2:
+                    z_send(k, -step)
         for j, xk in enumerate(XPEERS):
             seen = XPEERS.index(NX - xk)
             remote(block, block, sem_x_send.at[j], sem_x.at[seen, slot], at_x(xk)).start()
         share(k, x)
 
-    def x_steps(g):
-        for slot in range(4 * g, 4 * g + 4) if g < 2 else range(4 * g + 3, 4 * g - 1, -1):
-            for j, xk in enumerate(XPEERS):
-                px = lax.rem(x + xk, NX)
-                block = spot(tokens, slot, px)
-                remote(block, block, sem_x_send.at[j], sem_x.at[j, slot], partner).wait_recv()
-                share(slot, px)
+    def x_step(slot):
+        for j, xk in enumerate(XPEERS):
+            px = lax.rem(x + xk, NX)
+            block = spot(tokens, slot, px)
+            remote(block, block, sem_x_send.at[j], sem_x.at[j, slot], partner).wait_recv()
+            share(slot, px)
 
     def rows_of(g):
         return slice(g * CHUNK, (g + 1) * CHUNK)
@@ -246,20 +214,68 @@
     for k in range(REACH, 0, -1):
         z_send(0, k)
         z_send(0, -k)
-    for k in ZORDER:
+    z_step(0)
+
+    for k in ZORDER[1:5]:
+        z_step(k)
+
+    for load in loads[1:4]:
+        load.wait()
+    lane = lax.broadcasted_iota(I32, (1, TOK), 1)
+    lane_x, lane_z = (lane >> 4) & 3, (z + (lane >> 6)) & (NZ - 1)
+    place = ((lane_z & 1) << 6) + (((lane >> 3) & 1) << 5) + (lane & 7)
+    ids = targets[...]
+    digits = jnp.concatenate([ids & 255, (ids >> 8) & 255, ids >> 16], axis=0).astype(F32).astype(BF16)
+    here = lax.broadcasted_iota(I32, (32, TOK), 0) == lane_x * 8 + (lane_z >> 1)
+
+    def plane_targets(py):
+        pick = lax.broadcasted_iota(I32, (128, TOK), 0) == place + py * 8
+        found = dot(digits, pick.astype(F32).astype(BF16), ((1,), (0,)))
+        value = found[:32] + found[32:64] * 256.0 + found[64:] * 65536.0
+        return jnp.sum(jnp.where(here, value, 0.0), axis=0, keepdims=True).astype(I32)
+
+    own_targets = plane_targets(y)
+    other_targets = plane_targets(lax.rem(y + 2, NY))
+    rows[0:1, :] = own_targets
+    rows[1:2, :] = other_targets
+
+    for k in ZORDER[5:9]:
+        z_step(k)
+    x_step(0)
+
+    sentence = lax.broadcasted_iota(I32, (64, TOK), 0) == lane_x * NZ + lane_z
+    lang = dot(
+        jnp.broadcast_to(sent[...], (8, 64)).astype(F32).astype(BF16),
+        sentence.astype(F32).astype(BF16), ((1,), (0,)),
+    )[0:1].astype(I32)
+    lists_now = lists[...]
+    member = jnp.concatenate(
+        [jnp.any(lists_now == v * NB + b, axis=0, keepdims=True).astype(F32) for b in range(NB)],
+        axis=0,
+    )
+    hit = (lax.broadcasted_iota(I32, (lists.shape[1], TOK), 0) == lang).astype(F32)
+    allowed[...] = dot(member, hit, ((1,), (0,)))
+
+    for slot in (1, 15, 2, 14):
+        x_step(slot)
+    for k in ZORDER[9:13]:
+        z_step(k)
+    for slot in (3, 13, 4, 12):
+        x_step(slot)
+    for k in ZORDER[13:]:
         z_step(k)
     loads[4].wait()
     loads[5].wait()
     log_counts = jnp.log(counts[...].astype(F32))
 
     ca, cb, cc, cd = CHUNKS
-    x_steps(ca)
-    x_steps(cb)
     chunk_logits(ca)
-    x_steps(cc)
+    for slot in (5, 11, 6, 10):
+        x_step(slot)
     chunk_logits(cb)
     chunk_totals(ca)
-    x_steps(cd)
+    for slot in (7, 9, 8):
+        x_step(slot)
     chunk_logits(cc)
     chunk_totals(cb)
     chunk_logits(cd)
@@ -307,6 +323,15 @@
     other_logits(cb)
     pass_on(cd)
     other_logits(cc)
+    tsum = tgt_out[...]
+    for i, (k, f) in enumerate(XC_PEERS):
+        there = slot_of(k, f)
+        remote(tgt_out, t1.at[there], sem_t1s.at[i], sem_t1.at[there], partner).wait_recv()
+        tsum = tsum + t1[there]
+    tsum_out[...] = tsum
+    for k in far_first:
+        remote(tsum_out.at[k // 2], t2.at[z], sem_t2s.at[k], sem_t2.at[z], at_z(k)).start()
+    other_logits(cd)
 
     first_half = lax.broadcasted_iota(I32, (1, 128), 1) < 64
     parts = [[l1_out[r]] for r in range(8)]
@@ -331,7 +356,6 @@
         l_out[r] = total_rows[r]
     tell = remote(l_out, l_in, sem_l.at[0], sem_l.at[1], across)
     tell.start()
-    other_logits(cd)
 
     scale = jnp.exp(jnp.concatenate(peaks, axis=1) - jnp.concatenate(total_rows, axis=1))
     deep = lax.broadcasted_iota(I32, (BLK, TOK), 0)
@@ -350,23 +374,16 @@
     tell.wait_recv()
     other_total = jnp.concatenate([l_in[r] for r in range(8)], axis=1)
     scale2 = jnp.exp(jnp.concatenate(peaks2, axis=1) - other_total)
-    for n, b in enumerate(held_blocks):
-        fill_probs(logits2, n, b, n, scale2, other_row)
     for n, to in ((0, at_y(1)), (1, at_y(3))):
+        fill_probs(logits2, n, held_blocks[n], n, scale2, other_row)
         at = slice(n * BLK, (n + 1) * BLK)
         send_buf[n] = (sums[at, :] + dot(probs[at, :], tokens2[...], ((1,), (0,)))).astype(BF16)
-        remote(send_buf.at[n], recv_buf.at[n], sem_rs.at[n], sem_rr.at[n], to).start()
-
-    tsum = tgt_out[...]
-    for i, (k, f) in enumerate(XC_PEERS):
-        there = slot_of(k, f)
-        remote(tgt_out, t1.at[there], sem_t1s.at[i], sem_t1.at[there], partner).wait_recv()
-        tsum = tsum + t1[there]
-    tsum_out[...] = tsum
-    for k in far_first:
-        remote(tsum_out.at[k // 2], t2.at[z], sem_t2s.at[k], sem_t2.at[z], at_z(k)).start()
-
+        remote(send_buf.at[n], recv_ref.at[pl.ds(n * BLK, BLK)], sem_rs.at[n], sem_rr.at[n], to).start()
+    for n in (2, 3):
+        fill_probs(logits2, n, held_blocks[n], n, scale2, other_row)
     sums[2 * BLK:, :] += dot(probs[2 * BLK:, :], tokens2[...], ((1,), (0,)))
+    put = pltpu.make_async_copy(sums.at[pl.ds(2 * BLK, QROWS)], own_ref, sem_out)
+    put.start()
 
     tgt = tsum_out[0]
     for k in far_first[::-1]:
@@ -379,11 +396,8 @@
     loss_ref[...] = pltpu.roll(loss, lax.rem(128 - lane0, 128), 1)
 
     for n in range(2):
-        remote(send_buf.at[n], recv_buf.at[n], sem_rs.at[n], sem_rr.at[n], partner).wait_recv()
-        at = slice(n * BLK, (n + 1) * BLK)
-        out_buf[at, :] = (sums[(2 + n) * BLK:(3 + n) * BLK, :] + recv_buf[n].astype(F32)).astype(BF16)
-    put = pltpu.make_async_copy(out_buf, grad_ref, sem_out)
-    put.start()
+        part = recv_ref.at[pl.ds(n * BLK, BLK)]
+        remote(send_buf.at[n], part, sem_rs.at[n], sem_rr.at[n], partner).wait_recv()
 
     trade.wait_send()
     tell.wait_send()
@@ -406,26 +420,28 @@
     for k in range(1, NZ):
         remote(tsum_out.at[0], t2.at[0], sem_t2s.at[k], sem_t2.at[0], partner).wait_send()
     for n in range(2):
-        remote(send_buf.at[n], recv_buf.at[n], sem_rs.at[n], sem_rr.at[n], partner).wait_send()
+        part = recv_ref.at[pl.ds(n * BLK, BLK)]
+        remote(send_buf.at[n], part, sem_rs.at[n], sem_rr.at[n], partner).wait_send()
     put.wait()
 
 
 def body(hidden, embedding, block_counts, lang_blocks, sent_lang, targets):
     vmem, dma = pltpu.VMEM, pltpu.SemaphoreType.DMA
     anywhere = pl.BlockSpec(memory_space=pl.ANY)
-    loss, grad = pl.pallas_call(
+    loss, own, received = pl.pallas_call(
         kernel,
         out_shape=(
             jax.ShapeDtypeStruct((8, 128), F32),
+            jax.ShapeDtypeStruct((QROWS, D), F32),
             jax.ShapeDtypeStruct((QROWS, D), BF16),
         ),
         in_specs=[anywhere] * 6,
-        out_specs=(pl.BlockSpec(memory_space=pltpu.VMEM), anywhere),
+        out_specs=(pl.BlockSpec(memory_space=pltpu.VMEM), anywhere, anywhere),
         scratch_shapes=[
             vmem(hidden.shape, BF16),
             vmem((ROWS, D), BF16),
             vmem((1, NB), I32),
-            vmem(lang_blocks.shape, I32),
+            vmem(lang_blocks.shape[::-1], I32),
             vmem((1, 64), I32),
             vmem((32, 128), I32),
             vmem((TOK, D), BF16),
@@ -448,8 +464,6 @@
             vmem((8, 1, 128), F32),
             vmem((8, 1, 128), F32),
             vmem((2, BLK, D), BF16),
-            vmem((2, BLK, D), BF16),
-            vmem((QROWS, D), BF16),
             dma((6,)), dma((2,)), dma, dma((NZ,)), dma((3,)), dma((3, NZ)),
             dma((4,)), dma((4,)), dma((4,)), dma((4,)), dma((4,)), dma((4,)),
             dma((4, 7)), dma((4, 8)), dma((4, NZ)), dma((4, NZ)),
@@ -457,13 +471,13 @@
             dma((2,)), dma((2,)), dma((2,)), dma,
         ],
         compiler_params=pltpu.CompilerParams(
-            collective_id=0, has_side_effects=True, vmem_limit_bytes=56 << 20
+            collective_id=0, has_side_effects=True, vmem_limit_bytes=54 << 20
         ),
     )(
-        hidden, embedding, block_counts.reshape(1, NB), lang_blocks,
+        hidden, embedding, block_counts.reshape(1, NB), lang_blocks.T,
         sent_lang.reshape(1, 64), targets.reshape(32, 128),
     )
-    return loss[0, :8], grad
+    return loss[0, :8], (own + received.astype(F32)).astype(BF16)
 
 
 def solution(mesh):

time: 70.8 us -> 67.8 us (0.958)
  local copies, waits for them, and re-layouts: 4.63 us -> 1.2 us
  other arithmetic: 0 us -> 2.3 us
  Pallas kernels: 64.6 us -> 63 us
    unnamed x2 -> x0, local copies, waits for them, and re-layouts: 3.45 us -> none
    convert_element_type x0 -> x1, other arithmetic: none -> 2.3 us  [body(): return (loss[0, :8], (own + received.astype(F32)).astype(BF16))]
    pallas_call x1, Pallas kernels: 64.6 us -> 63 us  [body(): pl.pallas_call(kernel, out_shape=(jax.ShapeDtypeStruct((8, 128), F32), ja...]
where the time goes in v3:
time: 67.8 us; the launch traced here: 67.1 us
  Pallas kernels  63 us (93%)
  other arithmetic  2.3 us (3%)
  local copies, waits for them, and re-layouts  1.2 us (2%)
    pallas_call x1, Pallas kernels, body(): pl.pallas_call(kernel, out_shape=(jax.ShapeDtypeStruct((8, 128), F32), ja...  63 us
    convert_element_type x1, other arithmetic, body(): return (loss[0, :8], (own + received.astype(F32)).astype(BF16))  2.3 us

profile of v3, /device:TPU:1, one launch (start us, length us, event | category | flops | bytes accessed | tf_op | source)
XLA Modules:
  0.0 67.1 jit_solution(3676908409441385260)
XLA Ops:
  0.6 63.0 %shard_map.77 = (f32[8,128]{1,0:T(8,128)}, f32[256,1024]{1,0:T(8,128)}, bf16[256,1024]{1,0:T(8,128)(2,1)}) custom-call(bf16[8,1024]{1,0:T(8,128)(2,1)} %hid_hbm.1, bf16[1024,1024]{1,0:T(8,128)(2,1)} %emb_hbm.1, s32[1,8]{1,0:T(1,128)} %bitcast.8, s32[64,200]{1,0:T(8,128)} %bitcast.6, s32[1,64]{1,0:T(1,128)} %bitcast.9, s32[32,128]{1,0:T(8,128)} %bitcast.7), custom_call_target="tpu_custom_call" | custom-call | tf_op jit(solution)/shard_map/pallas_call | solution.py:431
  63.6 1.2 %slice_bitcast_fusion = f32[8]{0:T(128)} fusion(f32[8,128]{1,0:T(8,128)} %get-tuple-element.5), kind=kLoop, calls=%fused_computation.1 | loop fusion | bytes 64 | tf_op jit(solution)/shard_map/squeeze | solution.py:480
  64.8 2.3 %add_convert_fusion = bf16[256,1024]{1,0:T(8,128)(2,1)} fusion(f32[256,1024]{1,0:T(8,128)} %get-tuple-element.6, bf16[256,1024]{1,0:T(8,128)(2,1)} %get-tuple-element.7), kind=kLoop, calls=%fused_computation | loop fusion | flops 786432 | bytes 2097152 | tf_op jit(solution)/shard_map/convert_element_type | solution.py:480

commit v4 on v3

--- a/solution.py
+++ b/solution.py
@@ -46,7 +46,7 @@
 def kernel(
     hid_hbm, emb_hbm, counts_hbm, lists_hbm, sent_hbm, targets_hbm,
     loss_ref, own_ref, recv_ref,
-    hid, table, counts, lists, sent, targets,
+    hid, table, table2, counts, lists, sent, targets,
     tokens, tokens2, logits, logits2, probs, sums, swap, allowed, rows,
     s1, s2, t1, t2, lse_out, l1_out, tgt_out, tsum_out, l_out, l_in,
     send_buf,
@@ -97,6 +97,46 @@
     low, high = mine[:, :HALF], mine[:, HALF:]
     swap[0] = jnp.where(c == 0, high, low)
     kept = jnp.where(c == 0, low, high)
+    for load in loads[1:4]:
+        load.wait()
+    lane = lax.broadcasted_iota(I32, (1, TOK), 1)
+    lane_x, lane_z = (lane >> 4) & 3, (z + (lane >> 6)) & (NZ - 1)
+    place = ((lane_z & 1) << 6) + (((lane >> 3) & 1) << 5) + (lane & 7)
+    ids = targets[...]
+    digits = jnp.concatenate([ids & 255, (ids >> 8) & 255, ids >> 16], axis=0).astype(F32).astype(BF16)
+    here = lax.broadcasted_iota(I32, (32, TOK), 0) == lane_x * 8 + (lane_z >> 1)
+
+    def plane_targets(py):
+        pick = lax.broadcasted_iota(I32, (128, TOK), 0) == place + py * 8
+        found = dot(digits, pick.astype(F32).astype(BF16), ((1,), (0,)))
+        value = found[:32] + found[32:64] * 256.0 + found[64:] * 65536.0
+        return jnp.sum(jnp.where(here, value, 0.0), axis=0, keepdims=True).astype(I32)
+
+    own_targets = plane_targets(y)
+    other_targets = plane_targets(lax.rem(y + 2, NY))
+    rows[0:1, :] = own_targets
+    rows[1:2, :] = other_targets
+    sentence = lax.broadcasted_iota(I32, (64, TOK), 0) == lane_x * NZ + lane_z
+    lang = dot(
+        jnp.broadcast_to(sent[...], (8, 64)).astype(F32).astype(BF16),
+        sentence.astype(F32).astype(BF16), ((1,), (0,)),
+    )[0:1].astype(I32)
+    lists_now = lists[...]
+    member = jnp.concatenate(
+        [jnp.any(lists_now == v * NB + b, axis=0, keepdims=True).astype(F32) for b in range(NB)],
+        axis=0,
+    )
+    hit = (lax.broadcasted_iota(I32, (lists.shape[1], TOK), 0) == lang).astype(F32)
+    allowed[...] = dot(member, hit, ((1,), (0,)))
+    loads[4].wait()
+    loads[5].wait()
+    log_counts = jnp.log(counts[...].astype(F32))
+    up = lax.rem(y + 1, NY) * 2
+    down = lax.rem(y + 3, NY) * 2 + 1
+    held_blocks = (up, down, y * 2, y * 2 + 1)
+    for n, b in enumerate(held_blocks):
+        table2[n * BLK:(n + 1) * BLK, :] = table[pl.ds(pl.multiple_of(b * BLK, BLK), BLK), :]
+
     pl.semaphore_wait(barrier, len(near))
     trade = remote(swap.at[0], swap.at[1], sem_swap.at[0], sem_swap.at[1], partner)
     trade.start()
@@ -166,7 +206,9 @@
         top = jnp.full((1, CHUNK), FILL, F32)
         hit_logit = jnp.zeros((1, CHUNK), F32)
         for b in range(NB):
-            score = dot(table[b * BLK:(b + 1) * BLK, :], held, ((1,), (1,))) - log_counts[0:1, b:b + 1]
+            if b % 4 == 0:
+                raw = dot(table[b * BLK:(b + 4) * BLK, :], held, ((1,), (1,)))
+            score = raw[b % 4 * BLK:(b % 4 + 1) * BLK] - log_counts[0:1, b:b + 1]
             score = jnp.where(allowed[b:b + 1, at] > 0.5, score, FILL)
             logits[b * BLK:(b + 1) * BLK, at] = score
             top = jnp.maximum(top, jnp.max(score, axis=0, keepdims=True))
@@ -214,49 +256,9 @@
     for k in range(REACH, 0, -1):
         z_send(0, k)
         z_send(0, -k)
-    z_step(0)
-
-    for k in ZORDER[1:5]:
+    for k in ZORDER[:9]:
         z_step(k)
-
-    for load in loads[1:4]:
-        load.wait()
-    lane = lax.broadcasted_iota(I32, (1, TOK), 1)
-    lane_x, lane_z = (lane >> 4) & 3, (z + (lane >> 6)) & (NZ - 1)
-    place = ((lane_z & 1) << 6) + (((lane >> 3) & 1) << 5) + (lane & 7)
-    ids = targets[...]
-    digits = jnp.concatenate([ids & 255, (ids >> 8) & 255, ids >> 16], axis=0).astype(F32).astype(BF16)
-    here = lax.broadcasted_iota(I32, (32, TOK), 0) == lane_x * 8 + (lane_z >> 1)
-
-    def plane_targets(py):
-        pick = lax.broadcasted_iota(I32, (128, TOK), 0) == place + py * 8
-        found = dot(digits, pick.astype(F32).astype(BF16), ((1,), (0,)))
-        value = found[:32] + found[32:64] * 256.0 + found[64:] * 65536.0
-        return jnp.sum(jnp.where(here, value, 0.0), axis=0, keepdims=True).astype(I32)
-
-    own_targets = plane_targets(y)
-    other_targets = plane_targets(lax.rem(y + 2, NY))
-    rows[0:1, :] = own_targets
-    rows[1:2, :] = other_targets
-
-    for k in ZORDER[5:9]:
-        z_step(k)
-    x_step(0)
-
-    sentence = lax.broadcasted_iota(I32, (64, TOK), 0) == lane_x * NZ + lane_z
-    lang = dot(
-        jnp.broadcast_to(sent[...], (8, 64)).astype(F32).astype(BF16),
-        sentence.astype(F32).astype(BF16), ((1,), (0,)),
-    )[0:1].astype(I32)
-    lists_now = lists[...]
-    member = jnp.concatenate(
-        [jnp.any(lists_now == v * NB + b, axis=0, keepdims=True).astype(F32) for b in range(NB)],
-        axis=0,
-    )
-    hit = (lax.broadcasted_iota(I32, (lists.shape[1], TOK), 0) == lang).astype(F32)
-    allowed[...] = dot(member, hit, ((1,), (0,)))
-
-    for slot in (1, 15, 2, 14):
+    for slot in (0, 1, 15, 2, 14):
         x_step(slot)
     for k in ZORDER[9:13]:
         z_step(k)
@@ -264,9 +266,34 @@
         x_step(slot)
     for k in ZORDER[13:]:
         z_step(k)
-    loads[4].wait()
-    loads[5].wait()
-    log_counts = jnp.log(counts[...].astype(F32))
+
+    peaks2 = [None] * 4
+
+    def pass_on(g):
+        whole = chunk_of(tokens2, g)
+        remote(whole, whole, sem_y_send.at[g], sem_y.at[g], partner).wait_recv()
+        remote(whole, whole, sem_c2_send.at[g], sem_c2.at[g], partner).start()
+
+    block_lane = lax.broadcasted_iota(I32, (1, NB), 1)
+    block_row = lax.broadcasted_iota(I32, (NB, CHUNK), 0)
+
+    def other_logits(g):
+        whole = chunk_of(tokens2, g)
+        remote(whole, whole, sem_c2_send.at[g], sem_c2.at[g], partner).wait_recv()
+        at = rows_of(g)
+        held = tokens2[at, :]
+        may = allowed[:, at]
+        top = jnp.full((1, CHUNK), FILL, F32)
+        raw = dot(table2[...], held, ((1,), (1,)))
+        for i, b in enumerate(held_blocks):
+            less = jnp.sum(jnp.where(block_lane == b, log_counts, 0.0), axis=1, keepdims=True)
+            ok = jnp.sum(jnp.where(block_row == b, may, 0.0), axis=0, keepdims=True) > 0.5
+            score = jnp.where(ok, raw[i * BLK:(i + 1) * BLK] - less, FILL)
+            logits2[i * BLK:(i + 1) * BLK, at] = score
+            top = jnp.maximum(top, jnp.max(score, axis=0, keepdims=True))
+        for i in range(4):
+            logits2[i * BLK:(i + 1) * BLK, at] = jnp.exp(logits2[i * BLK:(i + 1) * BLK, at] - top)
+        peaks2[g] = top
 
     ca, cb, cc, cd = CHUNKS
     chunk_logits(ca)
@@ -278,47 +305,16 @@
         x_step(slot)
     chunk_logits(cc)
     chunk_totals(cb)
+    pass_on(ca)
     chunk_logits(cd)
     chunk_totals(cc)
+    other_logits(ca)
     chunk_totals(cd)
 
     for i, (k, f) in enumerate(XC_PEERS):
         remote(tgt_out, t1.at[my_slot], sem_t1s.at[i], sem_t1.at[my_slot], at_x(k, f)).start()
 
-    up = lax.rem(y + 1, NY) * 2
-    down = lax.rem(y + 3, NY) * 2 + 1
-    held_blocks = (up, down, y * 2, y * 2 + 1)
-    peaks2 = [None] * 4
-
-    def pass_on(g):
-        whole = chunk_of(tokens2, g)
-        remote(whole, whole, sem_y_send.at[g], sem_y.at[g], partner).wait_recv()
-        remote(whole, whole, sem_c2_send.at[g], sem_c2.at[g], partner).start()
-
-    block_lane = lax.broadcasted_iota(I32, (1, NB), 1)
-    block_row = lax.broadcasted_iota(I32, (NB, CHUNK), 0)
-
-    def other_logits(g):
-        whole = chunk_of(tokens2, g)
-        remote(whole, whole, sem_c2_send.at[g], sem_c2.at[g], partner).wait_recv()
-        at = rows_of(g)
-        held = tokens2[at, :]
-        may = allowed[:, at]
-        top = jnp.full((1, CHUNK), FILL, F32)
-        for i, b in enumerate(held_blocks):
-            entry = table[pl.ds(pl.multiple_of(b * BLK, BLK), BLK), :]
-            less = jnp.sum(jnp.where(block_lane == b, log_counts, 0.0), axis=1, keepdims=True)
-            ok = jnp.sum(jnp.where(block_row == b, may, 0.0), axis=0, keepdims=True) > 0.5
-            score = jnp.where(ok, dot(entry, held, ((1,), (1,))) - less, FILL)
-            logits2[i * BLK:(i + 1) * BLK, at] = score
-            top = jnp.maximum(top, jnp.max(score, axis=0, keepdims=True))
-        for i in range(4):
-            logits2[i * BLK:(i + 1) * BLK, at] = jnp.exp(logits2[i * BLK:(i + 1) * BLK, at] - top)
-        peaks2[g] = top
-
-    pass_on(ca)
     pass_on(cb)
-    other_logits(ca)
     pass_on(cc)
     other_logits(cb)
     pass_on(cd)
@@ -395,10 +391,6 @@
     loss = jnp.broadcast_to(l_out[0] - tgt, (8, 128))
     loss_ref[...] = pltpu.roll(loss, lax.rem(128 - lane0, 128), 1)
 
-    for n in range(2):
-        part = recv_ref.at[pl.ds(n * BLK, BLK)]
-        remote(send_buf.at[n], part, sem_rs.at[n], sem_rr.at[n], partner).wait_recv()
-
     trade.wait_send()
     tell.wait_send()
     block = tokens.at[pl.ds(0, 240), pl.ds(0, HALF)]
@@ -419,10 +411,10 @@
         remote(tgt_out, t1.at[0], sem_t1s.at[i], sem_t1.at[0], partner).wait_send()
     for k in range(1, NZ):
         remote(tsum_out.at[0], t2.at[0], sem_t2s.at[k], sem_t2.at[0], partner).wait_send()
+    put.wait()
     for n in range(2):
         part = recv_ref.at[pl.ds(n * BLK, BLK)]
-        remote(send_buf.at[n], part, sem_rs.at[n], sem_rr.at[n], partner).wait_send()
-    put.wait()
+        remote(send_buf.at[n], part, sem_rs.at[n], sem_rr.at[n], partner).wait()
 
 
 def body(hidden, embedding, block_counts, lang_blocks, sent_lang, targets):
@@ -440,6 +432,7 @@
         scratch_shapes=[
             vmem(hidden.shape, BF16),
             vmem((ROWS, D), BF16),
+            vmem((4 * BLK, D), BF16),
             vmem((1, NB), I32),
             vmem(lang_blocks.shape[::-1], I32),
             vmem((1, 64), I32),

time: 67.8 us -> 65.6 us (0.968)
  Pallas kernels: 63 us -> 60.8 us
    pallas_call x1, Pallas kernels: 63 us -> 60.8 us  [body(): pl.pallas_call(kernel, out_shape=(jax.ShapeDtypeStruct((8, 128), F32), ja...]
where the time goes in v4:
time: 65.6 us; the launch traced here: 64.9 us
  Pallas kernels  60.8 us (93%)
  other arithmetic  2.3 us (4%)
  local copies, waits for them, and re-layouts  1.2 us (2%)
    pallas_call x1, Pallas kernels, body(): pl.pallas_call(kernel, out_shape=(jax.ShapeDtypeStruct((8, 128), F32), ja...  60.8 us
    convert_element_type x1, other arithmetic, body(): return (loss[0, :8], (own + received.astype(F32)).astype(BF16))  2.3 us

profile of v4, /device:TPU:1, one launch (start us, length us, event | category | flops | bytes accessed | tf_op | source)
XLA Modules:
  0.0 64.9 jit_solution(1201657760209015827)
XLA Ops:
  0.6 60.8 %shard_map.77 = (f32[8,128]{1,0:T(8,128)}, f32[256,1024]{1,0:T(8,128)}, bf16[256,1024]{1,0:T(8,128)(2,1)}) custom-call(bf16[8,1024]{1,0:T(8,128)(2,1)} %hid_hbm.1, bf16[1024,1024]{1,0:T(8,128)(2,1)} %emb_hbm.1, s32[1,8]{1,0:T(1,128)} %bitcast.8, s32[64,200]{1,0:T(8,128)} %bitcast.6, s32[1,64]{1,0:T(1,128)} %bitcast.9, s32[32,128]{1,0:T(8,128)} %bitcast.7), custom_call_target="tpu_custom_call" | custom-call | tf_op jit(solution)/shard_map/pallas_call | solution.py:423
  61.4 1.2 %slice_bitcast_fusion = f32[8]{0:T(128)} fusion(f32[8,128]{1,0:T(8,128)} %get-tuple-element.5), kind=kLoop, calls=%fused_computation.1 | loop fusion | bytes 64 | tf_op jit(solution)/shard_map/squeeze | solution.py:473
  62.6 2.3 %add_convert_fusion = bf16[256,1024]{1,0:T(8,128)(2,1)} fusion(f32[256,1024]{1,0:T(8,128)} %get-tuple-element.6, bf16[256,1024]{1,0:T(8,128)(2,1)} %get-tuple-element.7), kind=kLoop, calls=%fused_computation | loop fusion | flops 786432 | bytes 2097152 | tf_op jit(solution)/shard_map/convert_element_type | solution.py:473

commit v5 on v4

--- a/solution.py
+++ b/solution.py
@@ -19,7 +19,7 @@
 QROWS = 256
 CHUNK = 256
 FILL = -3e38
-REACH = 2
+REACH = 3
 ZORDER = [0] + [s * k for k in range(1, 8) for s in (1, -1)] + [-8]
 XPEERS = (1, 3, 2)
 XC_PEERS = [(k, f) for f in (0, 1) for k in range(NX) if (k, f) != (0, 0)]
@@ -256,11 +256,11 @@
     for k in range(REACH, 0, -1):
         z_send(0, k)
         z_send(0, -k)
-    for k in ZORDER[:9]:
+    for k in ZORDER[:7]:
         z_step(k)
     for slot in (0, 1, 15, 2, 14):
         x_step(slot)
-    for k in ZORDER[9:13]:
+    for k in ZORDER[7:13]:
         z_step(k)
     for slot in (3, 13, 4, 12):
         x_step(slot)

time: 65.6 us -> 65.3 us (level)
  no operation moved by 1% of the time
where the time goes in v5:
time: 65.3 us; the launch traced here: 64.8 us
  Pallas kernels  60.6 us (93%)
  other arithmetic  2.3 us (4%)
  local copies, waits for them, and re-layouts  1.2 us (2%)
    pallas_call x1, Pallas kernels, body(): pl.pallas_call(kernel, out_shape=(jax.ShapeDtypeStruct((8, 128), F32), ja...  60.6 us
    convert_element_type x1, other arithmetic, body(): return (loss[0, :8], (own + received.astype(F32)).astype(BF16))  2.3 us

profile of v5, /device:TPU:1, one launch (start us, length us, event | category | flops | bytes accessed | tf_op | source)
XLA Modules:
  0.0 64.8 jit_solution(180919346813524328)
XLA Ops:
  0.6 60.6 %shard_map.77 = (f32[8,128]{1,0:T(8,128)}, f32[256,1024]{1,0:T(8,128)}, bf16[256,1024]{1,0:T(8,128)(2,1)}) custom-call(bf16[8,1024]{1,0:T(8,128)(2,1)} %hid_hbm.1, bf16[1024,1024]{1,0:T(8,128)(2,1)} %emb_hbm.1, s32[1,8]{1,0:T(1,128)} %bitcast.8, s32[64,200]{1,0:T(8,128)} %bitcast.6, s32[1,64]{1,0:T(1,128)} %bitcast.9, s32[32,128]{1,0:T(8,128)} %bitcast.7), custom_call_target="tpu_custom_call" | custom-call | tf_op jit(solution)/shard_map/pallas_call | solution.py:423
  61.3 1.2 %slice_bitcast_fusion = f32[8]{0:T(128)} fusion(f32[8,128]{1,0:T(8,128)} %get-tuple-element.5), kind=kLoop, calls=%fused_computation.1 | loop fusion | bytes 64 | tf_op jit(solution)/shard_map/squeeze | solution.py:473
  62.5 2.3 %add_convert_fusion = bf16[256,1024]{1,0:T(8,128)(2,1)} fusion(f32[256,1024]{1,0:T(8,128)} %get-tuple-element.6, bf16[256,1024]{1,0:T(8,128)(2,1)} %get-tuple-element.7), kind=kLoop, calls=%fused_computation | loop fusion | flops 786432 | bytes 2097152 | tf_op jit(solution)/shard_map/convert_element_type | solution.py:473

commit v6 on v5

--- a/solution.py
+++ b/solution.py
@@ -311,22 +311,11 @@
     other_logits(ca)
     chunk_totals(cd)
 
-    for i, (k, f) in enumerate(XC_PEERS):
-        remote(tgt_out, t1.at[my_slot], sem_t1s.at[i], sem_t1.at[my_slot], at_x(k, f)).start()
-
     pass_on(cb)
     pass_on(cc)
     other_logits(cb)
     pass_on(cd)
     other_logits(cc)
-    tsum = tgt_out[...]
-    for i, (k, f) in enumerate(XC_PEERS):
-        there = slot_of(k, f)
-        remote(tgt_out, t1.at[there], sem_t1s.at[i], sem_t1.at[there], partner).wait_recv()
-        tsum = tsum + t1[there]
-    tsum_out[...] = tsum
-    for k in far_first:
-        remote(tsum_out.at[k // 2], t2.at[z], sem_t2s.at[k], sem_t2.at[z], at_z(k)).start()
     other_logits(cd)
 
     first_half = lax.broadcasted_iota(I32, (1, 128), 1) < 64
@@ -352,6 +341,8 @@
         l_out[r] = total_rows[r]
     tell = remote(l_out, l_in, sem_l.at[0], sem_l.at[1], across)
     tell.start()
+    for i, (k, f) in enumerate(XC_PEERS):
+        remote(tgt_out, t1.at[my_slot], sem_t1s.at[i], sem_t1.at[my_slot], at_x(k, f)).start()
 
     scale = jnp.exp(jnp.concatenate(peaks, axis=1) - jnp.concatenate(total_rows, axis=1))
     deep = lax.broadcasted_iota(I32, (BLK, TOK), 0)
@@ -375,21 +366,19 @@
         at = slice(n * BLK, (n + 1) * BLK)
         send_buf[n] = (sums[at, :] + dot(probs[at, :], tokens2[...], ((1,), (0,)))).astype(BF16)
         remote(send_buf.at[n], recv_ref.at[pl.ds(n * BLK, BLK)], sem_rs.at[n], sem_rr.at[n], to).start()
+    tsum = tgt_out[...]
+    for i, (k, f) in enumerate(XC_PEERS):
+        there = slot_of(k, f)
+        remote(tgt_out, t1.at[there], sem_t1s.at[i], sem_t1.at[there], partner).wait_recv()
+        tsum = tsum + t1[there]
+    tsum_out[...] = tsum
+    for k in far_first:
+        remote(tsum_out.at[k // 2], t2.at[z], sem_t2s.at[k], sem_t2.at[z], at_z(k)).start()
     for n in (2, 3):
         fill_probs(logits2, n, held_blocks[n], n, scale2, other_row)
     sums[2 * BLK:, :] += dot(probs[2 * BLK:, :], tokens2[...], ((1,), (0,)))
     put = pltpu.make_async_copy(sums.at[pl.ds(2 * BLK, QROWS)], own_ref, sem_out)
     put.start()
-
-    tgt = tsum_out[0]
-    for k in far_first[::-1]:
-        there = lax.rem(z + k, NZ)
-        remote(tsum_out.at[0], t2.at[there], sem_t2s.at[k], sem_t2.at[there], partner).wait_recv()
-        theirs = t2[there]
-        tgt = tgt + (pltpu.roll(theirs, 64, 1) if k % 2 else theirs)
-    lane0 = x * 16 + c * 8
-    loss = jnp.broadcast_to(l_out[0] - tgt, (8, 128))
-    loss_ref[...] = pltpu.roll(loss, lax.rem(128 - lane0, 128), 1)
 
     trade.wait_send()
     tell.wait_send()
@@ -411,6 +400,15 @@
         remote(tgt_out, t1.at[0], sem_t1s.at[i], sem_t1.at[0], partner).wait_send()
     for k in range(1, NZ):
         remote(tsum_out.at[0], t2.at[0], sem_t2s.at[k], sem_t2.at[0], partner).wait_send()
+    tgt = tsum_out[0]
+    for k in far_first[::-1]:
+        there = lax.rem(z + k, NZ)
+        remote(tsum_out.at[0], t2.at[there], sem_t2s.at[k], sem_t2.at[there], partner).wait_recv()
+        theirs = t2[there]
+        tgt = tgt + (pltpu.roll(theirs, 64, 1) if k % 2 else theirs)
+    lane0 = x * 16 + c * 8
+    loss = jnp.broadcast_to(l_out[0] - tgt, (8, 128))
+    loss_ref[...] = pltpu.roll(loss, lax.rem(128 - lane0, 128), 1)
     put.wait()
     for n in range(2):
         part = recv_ref.at[pl.ds(n * BLK, BLK)]

time: 65.3 us -> 65.7 us (level)
  no operation moved by 1% of the time
where the time goes in v6:
time: 65.7 us; the launch traced here: 65.3 us
  Pallas kernels  61.1 us (93%)
  other arithmetic  2.3 us (4%)
  local copies, waits for them, and re-layouts  1.2 us (2%)
    pallas_call x1, Pallas kernels, body(): pl.pallas_call(kernel, out_shape=(jax.ShapeDtypeStruct((8, 128), F32), ja...  61.1 us
    convert_element_type x1, other arithmetic, body(): return (loss[0, :8], (own + received.astype(F32)).astype(BF16))  2.3 us

profile of v6, /device:TPU:1, one launch (start us, length us, event | category | flops | bytes accessed | tf_op | source)
XLA Modules:
  0.0 65.3 jit_solution(8368707519420988523)
XLA Ops:
  0.6 61.1 %shard_map.77 = (f32[8,128]{1,0:T(8,128)}, f32[256,1024]{1,0:T(8,128)}, bf16[256,1024]{1,0:T(8,128)(2,1)}) custom-call(bf16[8,1024]{1,0:T(8,128)(2,1)} %hid_hbm.1, bf16[1024,1024]{1,0:T(8,128)(2,1)} %emb_hbm.1, s32[1,8]{1,0:T(1,128)} %bitcast.8, s32[64,200]{1,0:T(8,128)} %bitcast.6, s32[1,64]{1,0:T(1,128)} %bitcast.9, s32[32,128]{1,0:T(8,128)} %bitcast.7), custom_call_target="tpu_custom_call" | custom-call | tf_op jit(solution)/shard_map/pallas_call | solution.py:421
  61.8 1.2 %slice_bitcast_fusion = f32[8]{0:T(128)} fusion(f32[8,128]{1,0:T(8,128)} %get-tuple-element.5), kind=kLoop, calls=%fused_computation.1 | loop fusion | bytes 64 | tf_op jit(solution)/shard_map/squeeze | solution.py:471
  63.0 2.3 %add_convert_fusion = bf16[256,1024]{1,0:T(8,128)(2,1)} fusion(f32[256,1024]{1,0:T(8,128)} %get-tuple-element.6, bf16[256,1024]{1,0:T(8,128)(2,1)} %get-tuple-element.7), kind=kLoop, calls=%fused_computation | loop fusion | flops 786432 | bytes 2097152 | tf_op jit(solution)/shard_map/convert_element_type | solution.py:471
